TPU v7x, 32 devices: a whole 2x2x4 slice. The times are simulated.
32 devices in a mesh: dp: 4 (over z), tensor: 8 (over y, x, core).
Axes of the slice: x: 2, y: 2, z: 4, core: 2. Of those that a mesh axis runs over, the one named last changes fastest.
Arguments:
- q_rows: bfloat16 [256, 1024], P('dp', 'tensor'), parts along dimension 0, may hold values from -160 to 160, as said below
- k_cache: bfloat16 [16, 2048, 512], P('dp', 'tensor'), parts along dimension 0, may hold values from -6 to 6
- v_cache: bfloat16 [16, 2048, 512], P('dp', 'tensor'), parts along dimension 0, may hold values from -24 to 24
- k_tree: bfloat16 [16, 16, 512], P('dp'), parts along dimension 0, may hold values from -18 to 18
- v_tree: bfloat16 [16, 16, 512], P('dp'), parts along dimension 0, may hold values from -24 to 24
- residual: bfloat16 [256, 8192], P('dp', 'tensor'), parts along dimension 0, may hold values from -2 to 2
- wo_rows: bfloat16 [1024, 8192], P('tensor'), may hold values from -1 to 1
- gain: bfloat16 [8192], P('tensor'), may hold values from 0.099609375 to 1.8984375
- parents: int32 [16, 16], P('dp'), parts along dimension 0, may hold values from 0 to 6, as said below
- cache_len: int32 [16], P('dp'), parts along dimension 0, may hold values from 256 to 2048, as said below
- accepted_node: int32 [16], P('dp'), parts along dimension 0, may hold values from 0 to 15, as said below
Outputs:
- layer_out: bfloat16 [256, 8192], P('dp', 'tensor'), parts along dimension 0
- draft_feat: bfloat16 [16, 8, 8192], P('dp', None, 'tensor'), parts along dimension 0
There are 4 independent parts, one for each index of `dp`. A program takes and returns all parts, laid end to end along the dimension named above; an argument that names none is the same for every part. Nothing has to cross between parts.
Inputs may be any that keep to these rules, and one draw needn't show every extreme that they name: `q_rows`: float queries of order one; in the hidden draw some rows are scaled up strongly. `parents`: nodes 1 to 7 form a chain (parent of node i is i - 1); every later node has a parent below 7; entry 0 is 0. `cache_len`: in every group some request has all 2048 positions valid. `accepted_node`: in every group some request accepts node 7, whose path holds 8 nodes.
All inputs are finite; a program needn't handle non-finite values.
Results may differ from a plain program's by a relative error of at most 0.0075.
Values may be sent and summed in bfloat16 or wider, within the bound.
A program may use at most 64 MiB of HBM per device.

v0:
```python
import jax
import jax.numpy as jnp
from jax import lax
from jax.sharding import PartitionSpec as P

HD = 128
HEADS_DEV = 1
KVH = 4
TREE = 16
MAXACC = 8


floor_score = -1e30
epsilon = 1e-05


def ancestors(parents):
    nodes = jnp.arange(TREE, dtype=jnp.int32)
    link = (parents[:, :, None] == nodes[None, None, :]) & (nodes[None, :, None] > 0)
    reach = jnp.minimum(jnp.eye(TREE, dtype=jnp.float32)[None] + link.astype(jnp.float32), 1.0)
    for sweep in range((TREE - 1).bit_length()):
        reach = jnp.minimum(
            jnp.einsum("rab,rbc->rac", reach, reach, precision=lax.Precision.HIGHEST), 1.0
        )
    return reach


def path_select(reach, accepted_node):
    depth = jnp.sum(reach, axis=2) - 1.0
    onehot = (jnp.arange(TREE, dtype=jnp.int32)[None, :] == accepted_node[:, None]).astype(
        jnp.float32
    )
    onpath = jnp.einsum("rt,rtu->ru", onehot, reach, precision=lax.Precision.HIGHEST)
    levels = jnp.arange(MAXACC).astype(jnp.float32)
    return onpath[:, None, :] * (depth[:, None, :] == levels[None, :, None]).astype(jnp.float32)


def combine(earlier, later):
    top = jnp.maximum(earlier[0], later[0])
    first = jnp.exp(earlier[0] - top)
    second = jnp.exp(later[0] - top)
    return (
        top,
        earlier[1] * first + later[1] * second,
        earlier[2] * first[..., None] + later[2] * second[..., None],
    )


def on_device(
    q_rows,
    k_cache,
    v_cache,
    k_tree,
    v_tree,
    residual,
    wo_rows,
    gain,
    parents,
    cache_len,
    accepted_node,
):
    rank_here = lax.axis_index("tensor")
    req_count, cache_dev, kv_width = k_cache.shape
    num_rows = q_rows.shape[0]
    tree_size = num_rows // req_count
    col_share = residual.shape[1]
    score_scale = HD ** (-0.5)
    q_all = lax.all_gather(q_rows, "tensor", axis=1, tiled=True)
    head_count = q_all.shape[1] // HD
    group_size = head_count // KVH
    q_view = q_all.reshape(req_count, tree_size, KVH, group_size, HD)
    cache_keys = k_cache.reshape(req_count, cache_dev, KVH, HD)
    cache_values = v_cache.reshape(req_count, cache_dev, KVH, HD)
    scores = (
        jnp.einsum("rtkgd,rckd->kgrtc", q_view, cache_keys, preferred_element_type=jnp.float32)
        * score_scale
    )
    positions = rank_here * cache_dev + jnp.arange(cache_dev, dtype=jnp.int32)
    valid = (positions[None, :] < cache_len[:, None])[None, None, :, None, :]
    local_max = jnp.max(jnp.where(valid, scores, floor_score), axis=4)
    weights = jnp.where(valid, jnp.exp(scores - local_max[..., None]), 0.0)
    local_sum = jnp.sum(weights, axis=4)
    local_acc = jnp.einsum(
        "kgrtc,rckd->kgrtd",
        weights.astype(jnp.bfloat16),
        cache_values,
        preferred_element_type=jnp.float32,
    )
    part_max = local_max.reshape(head_count, num_rows)
    part_sum = local_sum.reshape(head_count, num_rows)
    part_acc = local_acc.reshape(head_count, num_rows, HD)
    recv_max, recv_sum, recv_acc = (
        lax.all_to_all(part_max, "tensor", split_axis=0, concat_axis=0, tiled=True),
        lax.all_to_all(part_sum, "tensor", split_axis=0, concat_axis=0, tiled=True),
        lax.all_to_all(part_acc, "tensor", split_axis=0, concat_axis=0, tiled=True),
    )
    recv_max = recv_max.reshape(-1, HEADS_DEV, num_rows)
    recv_sum = recv_sum.reshape(-1, HEADS_DEV, num_rows)
    recv_acc = recv_acc.reshape(-1, HEADS_DEV, num_rows, HD)
    own_max = jnp.max(recv_max, axis=0)
    factor = jnp.exp(recv_max - own_max[None])
    own_sum = jnp.sum(recv_sum * factor, axis=0)
    own_acc = jnp.sum(recv_acc * factor[..., None], axis=0)
    reach = ancestors(parents)
    own_q = q_rows.reshape(req_count, tree_size, HEADS_DEV, HD)
    kv_index = rank_here * HEADS_DEV // group_size
    tree_keys = lax.dynamic_slice_in_dim(
        k_tree.reshape(req_count, tree_size, KVH, HD), kv_index, 1, 2
    )[:, :, 0]
    tree_values = lax.dynamic_slice_in_dim(
        v_tree.reshape(req_count, tree_size, KVH, HD), kv_index, 1, 2
    )[:, :, 0]
    tree_scores = (
        jnp.einsum("rtjd,rud->jrtu", own_q, tree_keys, preferred_element_type=jnp.float32)
        * score_scale
    )
    tree_valid = (reach > 0.5)[None]
    tree_max = jnp.max(jnp.where(tree_valid, tree_scores, floor_score), axis=3)
    tree_weights = jnp.where(tree_valid, jnp.exp(tree_scores - tree_max[..., None]), 0.0)
    tree_sum = jnp.sum(tree_weights, axis=3).reshape(HEADS_DEV, num_rows)
    tree_acc = jnp.einsum(
        "jrtu,rud->jrtd",
        tree_weights.astype(jnp.bfloat16),
        tree_values,
        preferred_element_type=jnp.float32,
    )
    joined = combine(
        (own_max, own_sum, own_acc),
        (
            tree_max.reshape(HEADS_DEV, num_rows),
            tree_sum,
            tree_acc.reshape(HEADS_DEV, num_rows, HD),
        ),
    )
    attention = (joined[2] / joined[1][..., None]).astype(jnp.bfloat16)
    attention = jnp.transpose(attention, (1, 0, 2)).reshape(num_rows, HEADS_DEV * HD)
    term = jnp.dot(attention, wo_rows, preferred_element_type=jnp.float32)
    own_cols = lax.dynamic_slice_in_dim(
        term, rank_here * col_share, col_share, 1
    ) + residual.astype(jnp.float32)
    term = lax.dynamic_update_slice_in_dim(term, own_cols, rank_here * col_share, 1)
    full_hidden = lax.psum(term, "tensor")
    mean_square = jnp.mean(full_hidden * full_hidden, axis=1)
    hidden = lax.dynamic_slice_in_dim(full_hidden, rank_here * col_share, col_share, 1)
    layer_out = hidden.astype(jnp.bfloat16)
    features = (
        hidden * lax.rsqrt(mean_square + epsilon)[:, None] * gain.astype(jnp.float32)[None, :]
    ).astype(jnp.bfloat16)
    select = path_select(reach, accepted_node).astype(jnp.bfloat16)
    draft_feat = jnp.einsum(
        "rat,rtc->rac",
        select,
        features.reshape(req_count, tree_size, col_share),
        preferred_element_type=jnp.float32,
    )
    return (layer_out, draft_feat.astype(jnp.bfloat16))


def solution(mesh):
    return jax.shard_map(
        on_device,
        mesh=mesh,
        in_specs=(
            P("dp", "tensor"),
            P("dp", "tensor", None),
            P("dp", "tensor", None),
            P("dp", None, None),
            P("dp", None, None),
            P("dp", "tensor"),
            P("tensor", None),
            P("tensor"),
            P("dp", None),
            P("dp"),
            P("dp"),
        ),
        out_specs=(P("dp", "tensor"), P("dp", None, "tensor")),
        check_vma=False,
    )
```

profile of v0, /device:TPU:0, one launch (start us, length us, event | category | flops | bytes accessed | tf_op | source)
XLA Modules:
  0.0 128.3 jit_solution(16946118198053912911)
XLA Ops:
  7.2 10.8 %all_gather.3 = bf16[64,1024]{1,0:T(8,128)(2,1)S(1)} all-gather(bf16[64,128]{1,0:T(8,128)(2,1)} %param.11), channel_id=1, replica_groups=mesh['dp'=4,'tensor'=8] {'tensor'}, dimensions={1}, use_global_device_ids=true | all-gather | bytes 147456 | tf_op jit(solution)/shard_map/all_gather | solution.py:68
  18.2 2.3 %reshape.248 = bf16[4,256,4,128]{3,2,1,0:T(4,128)(2,1)} reshape(bf16[4,256,512]{2,1,0:T(8,128)(2,1)} %param.12) | data formatting | bytes 2097152 | tf_op jit(solution)/shard_map/reshape | solution.py:72
  20.5 2.5 %select_reduce_fusion = (f32[4,2,4,16]{3,1,2,0:T(2,128)S(1)}, f32[4,2,4,16,256]{4,3,1,2,0:T(8,128)}) fusion(pred[4,256]{1,0:T(4,128)(4,1)S(1)} %broadcast_compare_fusion.1, bf16[4,16,4,2,128]{4,3,2,1,0:T(2,128)(2,1)S(1)} %reshape.249, bf16[4,256,4,128,1]{3,2,1,0,4:T(4,128)(2,1)} %bitcast.64), kind=kOutput, calls=%fused_computation.14 | convolution fusion | flops 33947136 | bytes 1707008 | tf_op jit(solution)/shard_map/rtkgd,rckd->kgrtc/dot_general | solution.py:75
  23.0 0.7 all_to_all.16
  23.7 3.3 %all-to-all-start.1 = ((f32[8,1,64]{2,1,0:T(1,128)}), f32[8,1,64]{2,1,0:T(1,128)S(1)}, u32[]{:S(2)}, u32[]{:S(2)}) async-start(f32[8,1,64]{2,1,0:T(1,128)} %bitcast.5), calls=%async_computation.1 | async-start | bytes 8192 | tf_op jit(solution)/shard_map/all_to_all | solution.py:93
  27.1 0.2 convolution_minimum_fusion.3
  27.7 0.2 fusion.46
  28.1 1.1 reshape.250
  29.2 1.8 %convolution_bitcast_fusion = f32[4,2,4,16,128]{4,3,1,2,0:T(8,128)S(1)} fusion(bf16[4,256,4,128,1]{3,2,1,0,4:T(4,128)(2,1)} %bitcast.65, f32[4,2,4,16,256]{4,3,1,2,0:T(8,128)} %get-tuple-element.11, f32[4,2,4,16]{3,1,2,0:T(2,128)S(1)} %get-tuple-element.10, pred[4,256]{1,0:T(4,128)(4,1)S(1)} %broadcast_compare_fusion.1), kind=kOutput, calls=%fused_computation.3 | convolution fusion | flops 33947648 | bytes 1838080 | tf_op jit(solution)/shard_map/kgrtc,rckd->kgrtd/dot_general | solution.py:83
  31.0 0.2 select_reduce_fusion.1
  31.4 0.3 fusion.4
  31.8 0.7 all_to_all.18
  32.4 4.1 %all-to-all-start.2 = ((f32[8,1,64]{2,1,0:T(1,128)}), f32[8,1,64]{2,1,0:T(1,128)S(1)}, u32[]{:S(2)}, u32[]{:S(2)}) async-start(f32[8,1,64]{2,1,0:T(1,128)} %bitcast.18), calls=%async_computation.2 | async-start | bytes 8192 | tf_op jit(solution)/shard_map/all_to_all | solution.py:94
  36.9 0.7 copy.42
  37.6 3.5 %all-to-all-done.2 = f32[8,1,64]{2,1,0:T(1,128)S(1)} async-done(((f32[8,1,64]{2,1,0:T(1,128)}), f32[8,1,64]{2,1,0:T(1,128)S(1)}, u32[]{:S(2)}, u32[]{:S(2)}) %all-to-all-start.2) | async-done | bytes 2080 | tf_op jit(solution)/shard_map/all_to_all | solution.py:94
  41.1 3.4 %all-to-all-start = ((f32[8,64,128]{2,1,0:T(8,128)}), f32[8,64,128]{2,1,0:T(8,128)S(1)}, u32[]{:S(2)}, u32[]{:S(2)}) async-start(f32[8,64,128]{2,1,0:T(8,128)} %bitcast.4), calls=%async_computation | async-start | bytes 524288 | tf_op jit(solution)/shard_map/all_to_all | solution.py:95
  44.7 6.8 %all-to-all-done = f32[8,64,128]{2,1,0:T(8,128)S(1)} async-done(((f32[8,64,128]{2,1,0:T(8,128)}), f32[8,64,128]{2,1,0:T(8,128)S(1)}, u32[]{:S(2)}, u32[]{:S(2)}) %all-to-all-start) | async-done | bytes 262176 | tf_op jit(solution)/shard_map/all_to_all | solution.py:95
  51.7 1.7 %fusion.47 = f32[64,8192]{1,0:T(8,128)} fusion(bf16[64,128]{1,0:T(8,128)(2,1)S(1)} %fusion.13, bf16[128,8192]{1,0:T(8,128)(2,1)S(1)} %copy-done), kind=kOutput, calls=%fused_computation.80 | convolution fusion | flops 134217728 | bytes 4210688 | tf_op jit(solution)/shard_map/dot_general | solution.py:137
  53.4 1.7 %add_dynamic-update-slice_fusion = f32[64,8192]{1,0:T(8,128)} fusion(f32[64,8192]{1,0:T(8,128)} %fusion.47, s32[]{:T(128)S(6)} %select_n.34, bf16[64,1024]{1,0:T(8,128)(2,1)S(1)} %copy-done.3), kind=kLoop, calls=%fused_computation.18 | loop fusion | flops 131072 | bytes 655364 | tf_op jit(solution)/shard_map/dynamic_update_slice | solution.py:141
  55.4 60.7 %all-reduce.2.cloned.1.call-done = f32[64,8192]{1,0:T(8,128)} async-done(((f32[64,8192]{1,0:T(8,128)}), f32[64,8192]{1,0:T(8,128)}) %all-reduce.2.cloned.1.call-update) | async-done | bytes 2097168 | tf_op jit(solution)/shard_map/psum | solution.py:142
  116.1 1.8 %multiply_reduce_fusion = f32[64]{0:T(128)S(1)} fusion(f32[64,8192]{1,0:T(8,128)} %all-reduce.2.cloned.1.call-done), kind=kLoop, calls=%fused_computation | loop fusion | flops 1048512 | bytes 2097408 | tf_op jit(solution)/shard_map/reduce_sum | solution.py:143
  117.9 1.1 multiply_convert_fusion
  119.0 0.8 convolution_convert_fusion
  119.8 1.6 %dynamic-slice_convert_fusion = bf16[64,1024]{1,0:T(8,128)(2,1)} fusion(f32[64,8192]{1,0:T(8,128)} %all-reduce.2.cloned.1.call-done, s32[]{:T(128)S(6)} %select_n.34), kind=kLoop, calls=%fused_computation.23 | loop fusion | bytes 262148 | tf_op jit(solution)/shard_map/convert_element_type | solution.py:145
  (53 shorter events, 1.8 us)
Async XLA Ops:
  7.2 44.5 %copy-start = (bf16[128,8192]{1,0:T(8,128)(2,1)S(1)}, bf16[128,8192]{1,0:T(8,128)(2,1)}, u32[]{:S(2)}) copy-start(bf16[128,8192]{1,0:T(8,128)(2,1)} %param.17) | copy-start | bytes 6291460
  7.2 13.2 %copy-start.8 = (s32[4]{0:T(128)S(1)}, s32[4]{0:T(128)}, u32[]{:S(2)}) copy-start(s32[4]{0:T(128)} %param.20) | copy-start | bytes 52
  18.1 9.0 %copy-start.9 = (s32[4,16]{1,0:T(4,128)S(1)}, s32[4,16]{1,0:T(4,128)}, u32[]{:S(2)}) copy-start(s32[4,16]{1,0:T(4,128)} %param.19) | copy-start | bytes 772
  18.1 9.8 %copy-start.4 = (bf16[4,16,512]{2,1,0:T(8,128)(2,1)S(1)}, bf16[4,16,512]{2,1,0:T(8,128)(2,1)}, u32[]{:S(2)}) copy-start(bf16[4,16,512]{2,1,0:T(8,128)(2,1)} %param.14) | copy-start | bytes 196612
  18.1 9.8 %copy-start.5 = (bf16[4,16,512]{2,1,0:T(8,128)(2,1)S(1)}, bf16[4,16,512]{2,1,0:T(8,128)(2,1)}, u32[]{:S(2)}) copy-start(bf16[4,16,512]{2,1,0:T(8,128)(2,1)} %param.15) | copy-start | bytes 196612
  18.1 9.9 %copy-start.1 = (bf16[4,256,512]{2,1,0:T(8,128)(2,1)S(1)}, bf16[4,256,512]{2,1,0:T(8,128)(2,1)}, u32[]{:S(2)}) copy-start(bf16[4,256,512]{2,1,0:T(8,128)(2,1)} %param.13) | copy-start | bytes 3145732
  23.7 8.8 %all-to-all-start.1 = ((f32[8,1,64]{2,1,0:T(1,128)}), f32[8,1,64]{2,1,0:T(1,128)S(1)}, u32[]{:S(2)}, u32[]{:S(2)}) async-start(f32[8,1,64]{2,1,0:T(1,128)} %bitcast.5), calls=%async_computation.1 | async-start | bytes 8192 | tf_op jit(solution)/shard_map/all_to_all | solution.py:93
  28.0 3.0 %copy-start.6 = (bf16[64,128]{1,0:T(8,128)(2,1)S(1)}, bf16[64,128]{1,0:T(8,128)(2,1)}, u32[]{:S(2)}) copy-start(bf16[64,128]{1,0:T(8,128)(2,1)} %param.11) | copy-start | bytes 49156
  29.2 2.2 %copy-start.2 = (f32[4,2,4,16,256]{4,3,1,2,0:T(8,128)S(1)}, f32[4,2,4,16,256]{4,3,1,2,0:T(8,128)}, u32[]{:S(2)}) copy-start(f32[4,2,4,16,256]{4,3,1,2,0:T(8,128)} %get-tuple-element.11) | copy-start | bytes 1572868
  32.4 8.7 %all-to-all-start.2 = ((f32[8,1,64]{2,1,0:T(1,128)}), f32[8,1,64]{2,1,0:T(1,128)S(1)}, u32[]{:S(2)}, u32[]{:S(2)}) async-start(f32[8,1,64]{2,1,0:T(1,128)} %bitcast.18), calls=%async_computation.2 | async-start | bytes 8192 | tf_op jit(solution)/shard_map/all_to_all | solution.py:94
  41.1 10.3 %all-to-all-start = ((f32[8,64,128]{2,1,0:T(8,128)}), f32[8,64,128]{2,1,0:T(8,128)S(1)}, u32[]{:S(2)}, u32[]{:S(2)}) async-start(f32[8,64,128]{2,1,0:T(8,128)} %bitcast.4), calls=%async_computation | async-start | bytes 524288 | tf_op jit(solution)/shard_map/all_to_all | solution.py:95
  44.6 71.5 %all-reduce.2.cloned.1.call-start = ((), (), s32[]{:S(2)}) async-start(), calls=%async_computation.3 | async-start | bytes 4194304 | tf_op jit(solution)/shard_map/psum | solution.py:142
  51.7 1.7 %copy-start.3 = (bf16[64,1024]{1,0:T(8,128)(2,1)S(1)}, bf16[64,1024]{1,0:T(8,128)(2,1)}, u32[]{:S(2)}) copy-start(bf16[64,1024]{1,0:T(8,128)(2,1)} %param.16) | copy-start | bytes 393220
  53.4 1.7 %copy-start.7 = (bf16[1024]{0:T(1024)(128)(2,1)S(1)}, bf16[1024]{0:T(1024)(128)(2,1)}, u32[]{:S(2)}) copy-start(bf16[1024]{0:T(1024)(128)(2,1)} %param.18) | copy-start | bytes 6148
  53.4 1.7 %copy-start.10 = (s32[4]{0:T(128)S(1)}, s32[4]{0:T(128)}, u32[]{:S(2)}) copy-start(s32[4]{0:T(128)} %param.21) | copy-start | bytes 52
Sparse Core Ops, SparseCore 0:
  55.2 60.8 all-reduce.1
where the time goes:
time: 129 us; the launch traced here: 128 us
  waiting for transfers between devices  71 us (55%)
  between operations  14.3 us (11%)
  starting transfers between devices  10.9 us (8%)
  blocking collectives  10.8 us (8%)
  matrix products  8.23 us (6%)
  local copies, waits for them, and re-layouts  7.53 us (6%)
  other arithmetic  5.5 us (4%)
    psum x1, waiting for transfers between devices, on_device(): full_hidden = lax.psum(term, 'tensor')  60.7 us
    all_gather x1, blocking collectives, on_device(): q_all = lax.all_gather(q_rows, 'tensor', axis=1, tiled=True)  10.8 us
    all_to_all x1, waiting for transfers between devices, on_device(): lax.all_to_all(part_acc, 'tensor', split_axis=0, concat_axis=0, tiled=True)  6.77 us
    all_to_all x1, starting transfers between devices, on_device(): lax.all_to_all(part_sum, 'tensor', split_axis=0, concat_axis=0, tiled=True)  4.11 us
    all_to_all x1, waiting for transfers between devices, on_device(): lax.all_to_all(part_sum, 'tensor', split_axis=0, concat_axis=0, tiled=True)  3.5 us
    all_to_all x1, starting transfers between devices, on_device(): lax.all_to_all(part_acc, 'tensor', split_axis=0, concat_axis=0, tiled=True)  3.41 us
    all_to_all x1, starting transfers between devices, on_device(): lax.all_to_all(part_max, 'tensor', split_axis=0, concat_axis=0, tiled=True)  3.31 us
  transfers between devices with their start and end apart: 4, of which 3 were waited for; matrix products, arithmetic and copies ran while one was open for 5% of the time, Pallas kernels for 0%

commit v1 on v0

v1 whole, which is shorter than its diff:
```python
import functools

import jax
import jax.numpy as jnp
from jax import lax
from jax.experimental import pallas as pl
from jax.experimental.pallas import tpu as pltpu
from jax.sharding import PartitionSpec as P

HD = 128
KVH = 4
TREE = 16
MAXACC = 8

FLOOR = -1e30
EPS = 1e-05
F32 = jnp.float32
BF16 = jnp.bfloat16
NT = (((1,), (1,)), ((), ()))


def matmul(a, b):
    return jnp.dot(a, b, preferred_element_type=F32)


def iota(shape, dim):
    return lax.broadcasted_iota(jnp.int32, shape, dim)


def tree_reach(parents, reqs):
    rows = reqs * TREE
    node = iota((TREE, TREE), 0)
    child = iota((TREE, TREE), 1)
    blocks = []
    for r in range(reqs):
        link = (parents[r : r + 1, :] == node) & (child > 0)
        blocks.append(jnp.where(link | (node == child), 1.0, 0.0))
    stacked = jnp.concatenate(blocks, axis=0).astype(BF16)
    spread = jnp.where(iota((TREE, rows), 1) % TREE == iota((TREE, rows), 0), 1.0, 0.0)
    same = iota((rows, rows), 0) // TREE == iota((rows, rows), 1) // TREE
    reach = jnp.where(same, jnp.minimum(matmul(stacked, spread.astype(BF16)), 1.0), 0.0)
    for _ in range((TREE - 1).bit_length()):
        half = reach.astype(BF16)
        reach = jnp.minimum(matmul(half, half), 1.0)
    return reach


def kernel(
    count,
    q_ref,
    k_ref,
    v_ref,
    kt_ref,
    vt_ref,
    res_ref,
    wo_ref,
    gain_ref,
    parents_ref,
    len_ref,
    acc_node_ref,
    out_ref,
    draft_ref,
    q_all,
    k_buf,
    v_buf,
    kt_buf,
    vt_buf,
    res_buf,
    wo_buf,
    acc_send,
    acc_recv,
    stat_send,
    stat_recv,
    att_buf,
    hid_send,
    hid_recv,
    sq_send,
    sq_recv,
    load_sem,
    wo_sem,
    q_ssem,
    q_rsem,
    acc_ssem,
    acc_rsem,
    stat_ssem,
    stat_rsem,
    wx_ssem,
    wx_rsem,
    att_ssem,
    att_rsem,
    hid_ssem,
    hid_rsem,
    sq_ssem,
    sq_rsem,
):
    me = lax.axis_index("tensor")
    parity = me % 2
    pair = me // 2
    partner = me + 1 - 2 * parity
    pairs = count // 2
    reqs, span, _ = k_ref.shape
    rows = reqs * TREE
    group = count // KVH
    grows = group * TREE
    cols = res_ref.shape[1]
    kv_col = pl.multiple_of((me // group) * HD, HD)

    def remote(src, dst, ssem, rsem, peer):
        return pltpu.make_async_remote_copy(
            src_ref=src,
            dst_ref=dst,
            send_sem=ssem,
            recv_sem=rsem,
            device_id={"tensor": peer},
            device_id_type=pl.DeviceIdType.MESH,
        )

    my_rows = pl.ds(pl.multiple_of(me * TREE, TREE), TREE)
    q_own = pltpu.make_async_copy(q_ref, q_all.at[:, my_rows, :], load_sem.at[0])
    q_own.start()
    k_copies = [
        pltpu.make_async_copy(k_ref.at[r], k_buf.at[r], load_sem.at[1 + r]) for r in range(reqs)
    ]
    v_copies = [
        pltpu.make_async_copy(v_ref.at[r], v_buf.at[r], load_sem.at[1 + reqs + r])
        for r in range(reqs)
    ]
    base = 1 + 2 * reqs
    kt_copy = pltpu.make_async_copy(kt_ref.at[:, :, pl.ds(kv_col, HD)], kt_buf, load_sem.at[base])
    vt_copy = pltpu.make_async_copy(
        vt_ref.at[:, :, pl.ds(kv_col, HD)], vt_buf, load_sem.at[base + 1]
    )
    res_copy = pltpu.make_async_copy(res_ref, res_buf, load_sem.at[base + 2])
    for copy in k_copies + v_copies + [kt_copy, vt_copy, res_copy]:
        copy.start()

    barrier = pltpu.get_barrier_semaphore()
    peers = [lax.rem(me + k, count) for k in range(1, count)]
    for peer in peers:
        pl.semaphore_signal(
            barrier, inc=1, device_id={"tensor": peer}, device_id_type=pl.DeviceIdType.MESH
        )
    q_own.wait()
    pl.semaphore_wait(barrier, count - 1)

    mine = q_all.at[:, my_rows, :]
    q_sends = [
        remote(mine, mine, q_ssem.at[k], q_rsem.at[k], peers[k]) for k in range(count - 1)
    ]
    for copy in q_sends:
        copy.start()

    def wo_block(b, who):
        first = pl.multiple_of((2 * b + who) * cols, 128)
        return wo_ref.at[:, pl.ds(first, cols)]

    wx = [
        remote(
            wo_block(b, 1 - parity), wo_buf.at[b, parity], wx_ssem.at[b], wx_rsem.at[b], partner
        )
        for b in range(pairs)
    ]
    wo_copies = [
        pltpu.make_async_copy(wo_block(b, parity), wo_buf.at[b, parity], wo_sem.at[b])
        for b in range(pairs)
    ]
    for copy in wx + wo_copies:
        copy.start()

    kt_copy.wait()
    vt_copy.wait()
    reach_t = tree_reach(parents_ref[...], reqs)
    eye = jnp.where(iota((rows, rows), 0) == iota((rows, rows), 1), 1.0, 0.0).astype(BF16)
    reach = lax.dot_general(eye, reach_t.astype(BF16), NT, preferred_element_type=F32)
    scale = HD ** (-0.5)
    q_mine = q_all[:, my_rows, :].reshape(rows, HD)
    tree_scores = (
        lax.dot_general(q_mine, kt_buf[...].reshape(rows, HD), NT, preferred_element_type=F32)
        * scale
    )
    tree_valid = reach > 0.5
    tree_max = jnp.max(jnp.where(tree_valid, tree_scores, FLOOR), axis=1, keepdims=True)
    tree_w = jnp.where(tree_valid, jnp.exp(tree_scores - tree_max), 0.0)
    tree_sum = jnp.sum(tree_w, axis=1, keepdims=True)
    tree_acc = matmul(tree_w.astype(BF16), vt_buf[...].reshape(rows, HD))

    depth = jnp.sum(reach_t, axis=0, keepdims=True) - 1.0
    slots = reqs * MAXACC
    slot = iota((slots, rows), 0)
    node = iota((slots, rows), 1)
    hit = jnp.zeros((slots, rows), F32)
    for r in range(reqs):
        target = acc_node_ref[r] + r * TREE
        hit = jnp.where((slot // MAXACC == r) & (node == target), 1.0, hit)
    on_path = matmul(hit.astype(BF16), reach.astype(BF16))
    level = (slot % MAXACC).astype(F32)
    select = jnp.where(depth == level, on_path, 0.0).astype(BF16)

    for copy in q_sends:
        copy.wait_recv()

    lane = iota((count * TREE, HD), 1)
    stats = jnp.zeros((count * TREE, HD), F32)
    position = iota((count * TREE, span), 1) + me * span
    for r in range(reqs):
        k_copies[r].wait()
        scores = jnp.concatenate(
            [
                lax.dot_general(
                    q_all[r, g * grows : (g + 1) * grows, :],
                    k_buf[r, :, g * HD : (g + 1) * HD],
                    NT,
                    preferred_element_type=F32,
                )
                for g in range(KVH)
            ],
            axis=0,
        )
        scores = jnp.where(position < len_ref[r], scores * scale, FLOOR)
        top = jnp.max(scores, axis=1, keepdims=True)
        weights = jnp.where(position < len_ref[r], jnp.exp(scores - top), 0.0)
        total = jnp.sum(weights, axis=1, keepdims=True)
        stats = jnp.where(lane == r, top, stats)
        stats = jnp.where(lane == reqs + r, total, stats)
        weights = weights.astype(BF16)
        v_copies[r].wait()
        for g in range(KVH):
            part = matmul(
                weights[g * grows : (g + 1) * grows, :], v_buf[r, :, g * HD : (g + 1) * HD]
            )
            acc_send[g * group : (g + 1) * group, r] = part.astype(BF16).reshape(group, TREE, HD)
    stat_send[...] = stats.reshape(count, TREE, HD)

    acc_sends, stat_sends = [], []
    for k in range(count - 1):
        peer = peers[k]
        stat_sends.append(
            remote(
                stat_send.at[peer], stat_recv.at[k], stat_ssem.at[k], stat_rsem.at[k], peer
            )
        )
        acc_sends.append(
            remote(acc_send.at[peer], acc_recv.at[k], acc_ssem.at[k], acc_rsem.at[k], peer)
        )
        stat_sends[k].start()
        acc_sends[k].start()

    for copy in stat_sends:
        copy.wait_recv()
    all_stats = [stat_send[me]] + [stat_recv[k] for k in range(count - 1)]
    tops = [jnp.concatenate([s[:, r : r + 1] for r in range(reqs)], axis=0) for s in all_stats]
    sums = [
        jnp.concatenate([s[:, reqs + r : reqs + r + 1] for r in range(reqs)], axis=0)
        for s in all_stats
    ]
    peak = tree_max
    for top in tops:
        peak = jnp.maximum(peak, top)
    factor = jnp.exp(tree_max - peak)
    denominator = tree_sum * factor
    numerator = tree_acc * factor
    for k in range(count):
        factor = jnp.exp(tops[k] - peak)
        denominator = denominator + sums[k] * factor
        if k == 0:
            part = acc_send[me]
        else:
            acc_sends[k - 1].wait_recv()
            part = acc_recv[k - 1]
        numerator = numerator + part.reshape(rows, HD).astype(F32) * factor
    att_buf[parity] = (numerator / denominator).astype(BF16)

    att_copy = remote(
        att_buf.at[parity], att_buf.at[parity], att_ssem.at[0], att_rsem.at[0], partner
    )
    att_copy.start()
    for copy in wx:
        copy.wait_recv()
    for copy in wo_copies:
        copy.wait()
    att_copy.wait_recv()
    attention = jnp.concatenate([att_buf[0], att_buf[1]], axis=1)

    hid_sends = []
    for k in range(1, pairs):
        b = lax.rem(pair + pairs - k, pairs)
        hid_send[k - 1] = matmul(attention, wo_buf[b].reshape(2 * HD, cols)).astype(BF16)
        copy = remote(
            hid_send.at[k - 1],
            hid_recv.at[k - 1],
            hid_ssem.at[k - 1],
            hid_rsem.at[k - 1],
            2 * b + parity,
        )
        copy.start()
        hid_sends.append(copy)
    hidden = matmul(attention, wo_buf[pair].reshape(2 * HD, cols))
    res_copy.wait()
    hidden = hidden + res_buf[...].astype(F32)
    for k in range(pairs - 1):
        hid_sends[k].wait_recv()
        hidden = hidden + hid_recv[k].astype(F32)

    square = jnp.sum(hidden * hidden, axis=1, keepdims=True)
    diagonal = iota((rows, HD), 0) == iota((rows, HD), 1)
    sq_send[...] = jnp.broadcast_to(
        jnp.sum(jnp.where(diagonal, square, 0.0), axis=0, keepdims=True), (8, HD)
    )
    sq_sends = [
        remote(sq_send, sq_recv.at[k], sq_ssem.at[k], sq_rsem.at[k], peers[k])
        for k in range(count - 1)
    ]
    for copy in sq_sends:
        copy.start()
    out_ref[...] = hidden.astype(BF16)
    scaled = hidden * gain_ref[...].astype(F32)
    total = sq_send[...]
    for k in range(count - 1):
        sq_sends[k].wait_recv()
        total = total + sq_recv[k]
    mean = jnp.sum(jnp.where(diagonal, total[0:1, :], 0.0), axis=1, keepdims=True) / (cols * count)
    features = (scaled * lax.rsqrt(mean + EPS)).astype(BF16)
    draft_ref[...] = matmul(select, features).astype(BF16).reshape(reqs, MAXACC, cols)

    for copies in (q_sends, wx, stat_sends, acc_sends, [att_copy], hid_sends, sq_sends):
        for copy in copies:
            copy.wait_send()


def on_device(
    count,
    q_rows,
    k_cache,
    v_cache,
    k_tree,
    v_tree,
    residual,
    wo_rows,
    gain,
    parents,
    cache_len,
    accepted_node,
):
    reqs, span, width = k_cache.shape
    rows, cols = residual.shape
    pairs = count // 2
    hbm = pl.BlockSpec(memory_space=pl.ANY)
    vmem = pl.BlockSpec(memory_space=pltpu.VMEM)
    smem = pl.BlockSpec(memory_space=pltpu.SMEM)
    dma = pltpu.SemaphoreType.DMA
    others = count - 1
    return pl.pallas_call(
        functools.partial(kernel, count),
        out_shape=(
            jax.ShapeDtypeStruct((rows, cols), BF16),
            jax.ShapeDtypeStruct((reqs, MAXACC, cols), BF16),
        ),
        in_specs=[hbm] * 7 + [vmem, vmem, smem, smem],
        out_specs=(vmem, vmem),
        scratch_shapes=[
            pltpu.VMEM((reqs, count * TREE, HD), BF16),
            pltpu.VMEM((reqs, span, width), BF16),
            pltpu.VMEM((reqs, span, width), BF16),
            pltpu.VMEM((reqs, TREE, HD), BF16),
            pltpu.VMEM((reqs, TREE, HD), BF16),
            pltpu.VMEM((rows, cols), BF16),
            pltpu.VMEM((pairs, 2, HD, cols), BF16),
            pltpu.VMEM((count, reqs, TREE, HD), BF16),
            pltpu.VMEM((others, reqs, TREE, HD), BF16),
            pltpu.VMEM((count, TREE, HD), F32),
            pltpu.VMEM((others, TREE, HD), F32),
            pltpu.VMEM((2, rows, HD), BF16),
            pltpu.VMEM((pairs - 1, rows, cols), BF16),
            pltpu.VMEM((pairs - 1, rows, cols), BF16),
            pltpu.VMEM((8, HD), F32),
            pltpu.VMEM((others, 8, HD), F32),
            dma((4 + 2 * reqs,)),
            dma((pairs,)),
            dma((others,)),
            dma((others,)),
            dma((others,)),
            dma((others,)),
            dma((others,)),
            dma((others,)),
            dma((pairs,)),
            dma((pairs,)),
            dma((1,)),
            dma((1,)),
            dma((pairs - 1,)),
            dma((pairs - 1,)),
            dma((others,)),
            dma((others,)),
        ],
        compiler_params=pltpu.CompilerParams(
            collective_id=0, has_side_effects=True, vmem_limit_bytes=56 * 2**20
        ),
        name="verify",
    )(
        q_rows.reshape(reqs, TREE, HD),
        k_cache,
        v_cache,
        k_tree,
        v_tree,
        residual,
        wo_rows,
        gain.reshape(1, cols),
        parents,
        cache_len,
        accepted_node,
    )


def solution(mesh):
    return jax.shard_map(
        functools.partial(on_device, mesh.shape["tensor"]),
        mesh=mesh,
        in_specs=(
            P("dp", "tensor"),
            P("dp", "tensor", None),
            P("dp", "tensor", None),
            P("dp", None, None),
            P("dp", None, None),
            P("dp", "tensor"),
            P("tensor", None),
            P("tensor"),
            P("dp", None),
            P("dp"),
            P("dp"),
        ),
        out_specs=(P("dp", "tensor"), P("dp", None, "tensor")),
        check_vma=False,
    )
```

time: 129 us -> 34.6 us (0.27)
  waiting for transfers between devices: 71 us -> 0 us
  Pallas kernels: 0 us -> 29.4 us
  between operations: 14.3 us -> 0.64 us
  starting transfers between devices: 10.9 us -> 0 us
  blocking collectives: 10.8 us -> 0 us
  matrix products: 8.23 us -> 0 us
  other arithmetic: 5.5 us -> 0 us
  local copies, waits for them, and re-layouts: 7.53 us -> 4.32 us
    psum x1 -> x0, waiting for transfers between devices: 60.7 us -> none  [on_device(): full_hidden = lax.psum(term, 'tensor')]
    pallas_call x0 -> x1, Pallas kernels: none -> 29.4 us  [on_device(): pl.pallas_call(functools.partial(kernel, count), out_shape=(jax.ShapeDtyp...]
    all_to_all x3 -> x0, starting transfers between devices: 10.8 us -> none  [the longest x1 4.11 us: on_device(): lax.all_to_all(part_sum, 'tensor', split_axis=0, concat_axis=0, tiled=True)]
    all_gather x1 -> x0, blocking collectives: 10.8 us -> none  [on_device(): q_all = lax.all_gather(q_rows, 'tensor', axis=1, tiled=True)]
    all_to_all x3 -> x0, waiting for transfers between devices: 10.3 us -> none  [the longest x1 6.77 us: on_device(): lax.all_to_all(part_acc, 'tensor', split_axis=0, concat_axis=0, tiled=True)]
    dot_general x11 -> x0, matrix products: 8.23 us -> none  [the longest x1 2.52 us: on_device(): jnp.einsum('rtkgd,rckd->kgrtc', q_view, cache_keys, preferred_element_typ...]
    unnamed x22 -> x2, local copies, waits for them, and re-layouts: 0.06 us -> 3.04 us
    reduce_sum x5 -> x0, other arithmetic: 2.45 us -> none  [the longest x1 1.83 us: on_device(): mean_square = jnp.mean(full_hidden * full_hidden, axis=1)]
  transfers between devices with their start and end apart: 4 -> 0, of which waited for: 3 -> 0; matrix products, arithmetic and copies ran while one was open for 5% -> 0% of each run, Pallas kernels for 0% -> 0%
where the time goes in v1:
time: 34.6 us; the launch traced here: 34.3 us
  Pallas kernels  29.4 us (85%)
  local copies, waits for them, and re-layouts  4.32 us (12%)
  between operations  0.64 us (2%)
    pallas_call x1, Pallas kernels, on_device(): pl.pallas_call(functools.partial(kernel, count), out_shape=(jax.ShapeDtyp...  29.4 us
    unnamed x2, local copies, waits for them, and re-layouts  3.04 us
    reshape x1, local copies, waits for them, and re-layouts, on_device(): gain.reshape(1, cols)  1.28 us

profile of v1, /device:TPU:0, one launch (start us, length us, event | category | flops | bytes accessed | tf_op | source)
XLA Modules:
  0.0 34.3 jit_solution(16389023610843073287)
XLA Ops:
  0.6 1.3 %reshape.11.gain_ref = bf16[1,1024]{1,0:T(2,128)(2,1)} reshape(bf16[1024]{0:T(1024)(128)(2,1)} %param.18) | data formatting | bytes 4096 | tf_op jit(solution)/shard_map/reshape | solution.py:406
  1.9 29.4 %verify.1 = (bf16[64,1024]{1,0:T(8,128)(2,1)}, bf16[4,8,1024]{2,1,0:T(8,128)(2,1)}) custom-call(bf16[4,16,128]{2,1,0:T(8,128)(2,1)} %bitcast.1, bf16[4,256,512]{2,1,0:T(8,128)(2,1)} %k_ref.1, bf16[4,256,512]{2,1,0:T(8,128)(2,1)} %v_ref.1, bf16[4,16,512]{2,1,0:T(8,128)(2,1)} %kt_ref.1, bf16[4,16,512]{2,1,0:T(8,128)(2,1)} %vt_ref.1, bf16[64,1024]{1,0:T(8,128)(2,1)} %res_ref.1, ...), custom_call_target="tpu_custom_call" | custom-call | tf_op jit(solution)/shard_map/verify/pallas_call | solution.py:352
  31.3 1.6 %copy.15 = bf16[64,1024]{1,0:T(8,128)(2,1)} copy(bf16[64,1024]{1,0:T(8,128)(2,1)} %get-tuple-element.4) | data formatting | bytes 262144
  32.8 1.5 %copy.16 = bf16[4,8,1024]{2,1,0:T(8,128)(2,1)} copy(bf16[4,8,1024]{2,1,0:T(8,128)(2,1)} %get-tuple-element.5) | data formatting | bytes 131072

commit v2 on v1

--- a/solution.py
+++ b/solution.py
@@ -17,6 +17,17 @@
 F32 = jnp.float32
 BF16 = jnp.bfloat16
 NT = (((1,), (1,)), ((), ()))
+
+
+def parts(x):
+    high = x.astype(BF16)
+    rest = x - high.astype(F32)
+    mid = rest.astype(BF16)
+    return high, mid, (rest - mid.astype(F32)).astype(BF16)
+
+
+def full_columns(cols):
+    return max(128, cols // 4 // 128 * 128)
 
 
 def matmul(a, b):
@@ -57,9 +68,14 @@
     gain_ref,
     parents_ref,
     len_ref,
-    acc_node_ref,
+    node_ref,
+    out_hbm,
+    draft_hbm,
     out_ref,
     draft_ref,
+    parents_buf,
+    len_buf,
+    node_buf,
     q_all,
     k_buf,
     v_buf,
@@ -67,10 +83,9 @@
     vt_buf,
     res_buf,
     wo_buf,
+    wf_buf,
     acc_send,
     acc_recv,
-    stat_send,
-    stat_recv,
     att_buf,
     hid_send,
     hid_recv,
@@ -82,16 +97,17 @@
     q_rsem,
     acc_ssem,
     acc_rsem,
-    stat_ssem,
-    stat_rsem,
     wx_ssem,
     wx_rsem,
+    wf_ssem,
+    wf_rsem,
     att_ssem,
     att_rsem,
     hid_ssem,
     hid_rsem,
     sq_ssem,
     sq_rsem,
+    out_sem,
 ):
     me = lax.axis_index("tensor")
     parity = me % 2
@@ -103,6 +119,8 @@
     group = count // KVH
     grows = group * TREE
     cols = res_ref.shape[1]
+    full = wf_buf.shape[2]
+    some = cols - full
     kv_col = pl.multiple_of((me // group) * HD, HD)
 
     def remote(src, dst, ssem, rsem, peer):
@@ -115,6 +133,13 @@
             device_id_type=pl.DeviceIdType.MESH,
         )
 
+    barrier = pltpu.get_barrier_semaphore()
+    peers = [lax.rem(me + k, count) for k in range(1, count)]
+    for peer in peers:
+        pl.semaphore_signal(
+            barrier, inc=1, device_id={"tensor": peer}, device_id_type=pl.DeviceIdType.MESH
+        )
+
     my_rows = pl.ds(pl.multiple_of(me * TREE, TREE), TREE)
     q_own = pltpu.make_async_copy(q_ref, q_all.at[:, my_rows, :], load_sem.at[0])
     q_own.start()
@@ -131,15 +156,18 @@
         vt_ref.at[:, :, pl.ds(kv_col, HD)], vt_buf, load_sem.at[base + 1]
     )
     res_copy = pltpu.make_async_copy(res_ref, res_buf, load_sem.at[base + 2])
-    for copy in k_copies + v_copies + [kt_copy, vt_copy, res_copy]:
-        copy.start()
-
-    barrier = pltpu.get_barrier_semaphore()
-    peers = [lax.rem(me + k, count) for k in range(1, count)]
-    for peer in peers:
-        pl.semaphore_signal(
-            barrier, inc=1, device_id={"tensor": peer}, device_id_type=pl.DeviceIdType.MESH
-        )
+    small = [
+        pltpu.make_async_copy(src, dst, load_sem.at[base + 3 + i])
+        for i, (src, dst) in enumerate(
+            [
+                (parents_ref, parents_buf),
+                (node_ref, node_buf),
+                (len_ref, len_buf),
+            ]
+        )
+    ]
+    for copy in [kt_copy, vt_copy] + small + k_copies + v_copies + [res_copy]:
+        copy.start()
     q_own.wait()
     pl.semaphore_wait(barrier, count - 1)
 
@@ -152,7 +180,11 @@
 
     def wo_block(b, who):
         first = pl.multiple_of((2 * b + who) * cols, 128)
-        return wo_ref.at[:, pl.ds(first, cols)]
+        return wo_ref.at[:, pl.ds(first, some)]
+
+    def wo_full(owner):
+        first = pl.multiple_of(owner * cols + some, 128)
+        return wo_ref.at[:, pl.ds(first, full)]
 
     wx = [
         remote(
@@ -164,12 +196,17 @@
         pltpu.make_async_copy(wo_block(b, parity), wo_buf.at[b, parity], wo_sem.at[b])
         for b in range(pairs)
     ]
-    for copy in wx + wo_copies:
-        copy.start()
-
-    kt_copy.wait()
-    vt_copy.wait()
-    reach_t = tree_reach(parents_ref[...], reqs)
+    wf = [
+        remote(wo_full(peers[k]), wf_buf.at[me], wf_ssem.at[k], wf_rsem.at[k], peers[k])
+        for k in range(count - 1)
+    ]
+    wo_copies.append(pltpu.make_async_copy(wo_full(me), wf_buf.at[me], wo_sem.at[pairs]))
+    for copy in wf + wx + wo_copies:
+        copy.start()
+
+    for copy in [kt_copy, vt_copy] + small:
+        copy.wait()
+    reach_t = tree_reach(parents_buf[...], reqs)
     eye = jnp.where(iota((rows, rows), 0) == iota((rows, rows), 1), 1.0, 0.0).astype(BF16)
     reach = lax.dot_general(eye, reach_t.astype(BF16), NT, preferred_element_type=F32)
     scale = HD ** (-0.5)
@@ -190,7 +227,7 @@
     node = iota((slots, rows), 1)
     hit = jnp.zeros((slots, rows), F32)
     for r in range(reqs):
-        target = acc_node_ref[r] + r * TREE
+        target = node_buf[r] + r * TREE
         hit = jnp.where((slot // MAXACC == r) & (node == target), 1.0, hit)
     on_path = matmul(hit.astype(BF16), reach.astype(BF16))
     level = (slot % MAXACC).astype(F32)
@@ -200,7 +237,8 @@
         copy.wait_recv()
 
     lane = iota((count * TREE, HD), 1)
-    stats = jnp.zeros((count * TREE, HD), F32)
+    tops = jnp.full((count * TREE, HD), FLOOR, F32)
+    sums = jnp.zeros((count * TREE, HD), F32)
     position = iota((count * TREE, span), 1) + me * span
     for r in range(reqs):
         k_copies[r].wait()
@@ -216,12 +254,12 @@
             ],
             axis=0,
         )
-        scores = jnp.where(position < len_ref[r], scores * scale, FLOOR)
+        scores = jnp.where(position < len_buf[r], scores * scale, FLOOR)
         top = jnp.max(scores, axis=1, keepdims=True)
-        weights = jnp.where(position < len_ref[r], jnp.exp(scores - top), 0.0)
+        weights = jnp.where(position < len_buf[r], jnp.exp(scores - top), 0.0)
         total = jnp.sum(weights, axis=1, keepdims=True)
-        stats = jnp.where(lane == r, top, stats)
-        stats = jnp.where(lane == reqs + r, total, stats)
+        tops = jnp.where(lane == r, top, tops)
+        sums = jnp.where(lane == r, total, sums)
         weights = weights.astype(BF16)
         v_copies[r].wait()
         for g in range(KVH):
@@ -229,62 +267,81 @@
                 weights[g * grows : (g + 1) * grows, :], v_buf[r, :, g * HD : (g + 1) * HD]
             )
             acc_send[g * group : (g + 1) * group, r] = part.astype(BF16).reshape(group, TREE, HD)
-    stat_send[...] = stats.reshape(count, TREE, HD)
-
-    acc_sends, stat_sends = [], []
+    packed = jnp.zeros((count * TREE, HD), F32)
+    for i, piece in enumerate(parts(tops) + parts(sums)):
+        piece = piece.astype(F32)
+        if i:
+            piece = pltpu.roll(piece, i * reqs, 1)
+        packed = jnp.where(lane // reqs == i, piece, packed)
+    acc_send[:, reqs] = packed.astype(BF16).reshape(count, TREE, HD)
+
+    acc_sends = []
     for k in range(count - 1):
-        peer = peers[k]
-        stat_sends.append(
-            remote(
-                stat_send.at[peer], stat_recv.at[k], stat_ssem.at[k], stat_rsem.at[k], peer
-            )
-        )
-        acc_sends.append(
-            remote(acc_send.at[peer], acc_recv.at[k], acc_ssem.at[k], acc_rsem.at[k], peer)
-        )
-        stat_sends[k].start()
-        acc_sends[k].start()
-
-    for copy in stat_sends:
-        copy.wait_recv()
-    all_stats = [stat_send[me]] + [stat_recv[k] for k in range(count - 1)]
-    tops = [jnp.concatenate([s[:, r : r + 1] for r in range(reqs)], axis=0) for s in all_stats]
-    sums = [
-        jnp.concatenate([s[:, reqs + r : reqs + r + 1] for r in range(reqs)], axis=0)
-        for s in all_stats
-    ]
-    peak = tree_max
-    for top in tops:
-        peak = jnp.maximum(peak, top)
-    factor = jnp.exp(tree_max - peak)
-    denominator = tree_sum * factor
-    numerator = tree_acc * factor
+        copy = remote(
+            acc_send.at[peers[k]], acc_recv.at[k], acc_ssem.at[k], acc_rsem.at[k], peers[k]
+        )
+        copy.start()
+        acc_sends.append(copy)
+
+    small_lane = iota((TREE, HD), 1)
+
+    def as_lanes(column, fill):
+        wide = jnp.full((TREE, HD), fill, F32)
+        for r in range(reqs):
+            wide = jnp.where(small_lane == r, column[r * TREE : (r + 1) * TREE, :], wide)
+        return wide
+
+    def as_rows(wide):
+        return jnp.concatenate([wide[:, r : r + 1] for r in range(reqs)], axis=0)
+
+    def unpack(block):
+        block = block.astype(F32)
+        moved = [block] + [pltpu.roll(block, HD - i * reqs, 1) for i in range(1, 6)]
+        return moved[0] + moved[1] + moved[2], moved[3] + moved[4] + moved[5]
+
+    tops = [as_lanes(tree_max, 0.0)]
+    sums = [as_lanes(tree_sum, 1.0)]
     for k in range(count):
-        factor = jnp.exp(tops[k] - peak)
-        denominator = denominator + sums[k] * factor
-        if k == 0:
-            part = acc_send[me]
-        else:
+        if k:
             acc_sends[k - 1].wait_recv()
-            part = acc_recv[k - 1]
-        numerator = numerator + part.reshape(rows, HD).astype(F32) * factor
-    att_buf[parity] = (numerator / denominator).astype(BF16)
-
-    att_copy = remote(
-        att_buf.at[parity], att_buf.at[parity], att_ssem.at[0], att_rsem.at[0], partner
-    )
-    att_copy.start()
+        top, total = unpack(acc_recv[k - 1, reqs] if k else acc_send[me, reqs])
+        tops.append(jnp.where(small_lane < reqs, top, FLOOR))
+        sums.append(jnp.where(small_lane < reqs, total, 0.0))
+    peak = functools.reduce(jnp.maximum, tops)
+    factors = [jnp.exp(top - peak) for top in tops]
+    denominator = functools.reduce(
+        lambda a, b: a + b, [total * factor for total, factor in zip(sums, factors)]
+    )
+    inverse = 1.0 / denominator
+    attention = tree_acc * as_rows(factors[0] * inverse)
+    for k in range(count):
+        part = acc_recv[k - 1, pl.ds(0, reqs)] if k else acc_send[me, pl.ds(0, reqs)]
+        attention = attention + part.reshape(rows, HD).astype(F32) * as_rows(
+            factors[k + 1] * inverse
+        )
+    att_buf[me] = attention.astype(BF16)
+
+    att_peers = [partner]
+    for k in range(1, pairs):
+        first = 2 * lax.rem(pair + k, pairs)
+        att_peers += [first + parity, first + 1 - parity]
+    att_sends = [
+        remote(att_buf.at[me], att_buf.at[me], att_ssem.at[i], att_rsem.at[i], peer)
+        for i, peer in enumerate(att_peers)
+    ]
+    for copy in att_sends:
+        copy.start()
     for copy in wx:
         copy.wait_recv()
     for copy in wo_copies:
         copy.wait()
-    att_copy.wait_recv()
-    attention = jnp.concatenate([att_buf[0], att_buf[1]], axis=1)
+    att_sends[0].wait_recv()
+    attention = jnp.concatenate([att_buf[2 * pair], att_buf[2 * pair + 1]], axis=1)
 
     hid_sends = []
     for k in range(1, pairs):
         b = lax.rem(pair + pairs - k, pairs)
-        hid_send[k - 1] = matmul(attention, wo_buf[b].reshape(2 * HD, cols)).astype(BF16)
+        hid_send[k - 1] = matmul(attention, wo_buf[b].reshape(2 * HD, some)).astype(BF16)
         copy = remote(
             hid_send.at[k - 1],
             hid_recv.at[k - 1],
@@ -294,12 +351,19 @@
         )
         copy.start()
         hid_sends.append(copy)
-    hidden = matmul(attention, wo_buf[pair].reshape(2 * HD, cols))
+    hidden = matmul(attention, wo_buf[pair].reshape(2 * HD, some))
     res_copy.wait()
-    hidden = hidden + res_buf[...].astype(F32)
+    hidden = hidden + res_buf[:, :some].astype(F32)
+    for copy in wf:
+        copy.wait_recv()
+    for copy in att_sends[1:]:
+        copy.wait_recv()
+    attention = jnp.concatenate([att_buf[h] for h in range(count)], axis=1)
+    last = matmul(attention, wf_buf[...].reshape(count * HD, full)) + res_buf[:, some:].astype(F32)
     for k in range(pairs - 1):
         hid_sends[k].wait_recv()
         hidden = hidden + hid_recv[k].astype(F32)
+    hidden = jnp.concatenate([hidden, last], axis=1)
 
     square = jnp.sum(hidden * hidden, axis=1, keepdims=True)
     diagonal = iota((rows, HD), 0) == iota((rows, HD), 1)
@@ -313,18 +377,35 @@
     for copy in sq_sends:
         copy.start()
     out_ref[...] = hidden.astype(BF16)
-    scaled = hidden * gain_ref[...].astype(F32)
+    out_copy = pltpu.make_async_copy(out_ref, out_hbm, out_sem.at[0])
+    out_copy.start()
+    gain = gain_ref[...].astype(F32)
+    gain = jnp.concatenate([gain[i : i + 1, :] for i in range(cols // HD)], axis=1)
+    scaled = hidden * gain
     total = sq_send[...]
     for k in range(count - 1):
         sq_sends[k].wait_recv()
         total = total + sq_recv[k]
     mean = jnp.sum(jnp.where(diagonal, total[0:1, :], 0.0), axis=1, keepdims=True) / (cols * count)
     features = (scaled * lax.rsqrt(mean + EPS)).astype(BF16)
-    draft_ref[...] = matmul(select, features).astype(BF16).reshape(reqs, MAXACC, cols)
-
-    for copies in (q_sends, wx, stat_sends, acc_sends, [att_copy], hid_sends, sq_sends):
+    draft_ref[...] = matmul(select, features).astype(BF16)
+
+    draft_copy = pltpu.make_async_copy(draft_ref, draft_hbm, out_sem.at[1])
+    draft_copy.start()
+    for copies in (q_sends, wx, wf, acc_sends, att_sends, hid_sends, sq_sends):
         for copy in copies:
             copy.wait_send()
+    out_copy.wait()
+    draft_copy.wait()
+
+
+def hand_over(out_in, draft_in, out_ref, draft_ref, sem):
+    first = pltpu.make_async_copy(out_in, out_ref, sem.at[0])
+    second = pltpu.make_async_copy(draft_in, draft_ref, sem.at[1])
+    first.start()
+    second.start()
+    first.wait()
+    second.wait()
 
 
 def on_device(
@@ -346,50 +427,57 @@
     pairs = count // 2
     hbm = pl.BlockSpec(memory_space=pl.ANY)
     vmem = pl.BlockSpec(memory_space=pltpu.VMEM)
-    smem = pl.BlockSpec(memory_space=pltpu.SMEM)
     dma = pltpu.SemaphoreType.DMA
     others = count - 1
-    return pl.pallas_call(
+    full = full_columns(cols)
+    some = cols - full
+    out_shape = (
+        jax.ShapeDtypeStruct((rows, cols), BF16),
+        jax.ShapeDtypeStruct((reqs * MAXACC, cols), BF16),
+    )
+    results = pl.pallas_call(
         functools.partial(kernel, count),
-        out_shape=(
-            jax.ShapeDtypeStruct((rows, cols), BF16),
-            jax.ShapeDtypeStruct((reqs, MAXACC, cols), BF16),
-        ),
-        in_specs=[hbm] * 7 + [vmem, vmem, smem, smem],
-        out_specs=(vmem, vmem),
+        out_shape=out_shape,
+        in_specs=[hbm] * 7 + [vmem] + [hbm] * 3,
+        out_specs=(hbm, hbm),
         scratch_shapes=[
+            pltpu.VMEM((rows, cols), BF16),
+            pltpu.VMEM((reqs * MAXACC, cols), BF16),
+            pltpu.VMEM(parents.shape, jnp.int32),
+            pltpu.SMEM(cache_len.shape, jnp.int32),
+            pltpu.SMEM(accepted_node.shape, jnp.int32),
             pltpu.VMEM((reqs, count * TREE, HD), BF16),
             pltpu.VMEM((reqs, span, width), BF16),
             pltpu.VMEM((reqs, span, width), BF16),
             pltpu.VMEM((reqs, TREE, HD), BF16),
             pltpu.VMEM((reqs, TREE, HD), BF16),
             pltpu.VMEM((rows, cols), BF16),
-            pltpu.VMEM((pairs, 2, HD, cols), BF16),
-            pltpu.VMEM((count, reqs, TREE, HD), BF16),
-            pltpu.VMEM((others, reqs, TREE, HD), BF16),
-            pltpu.VMEM((count, TREE, HD), F32),
-            pltpu.VMEM((others, TREE, HD), F32),
-            pltpu.VMEM((2, rows, HD), BF16),
-            pltpu.VMEM((pairs - 1, rows, cols), BF16),
-            pltpu.VMEM((pairs - 1, rows, cols), BF16),
+            pltpu.VMEM((pairs, 2, HD, some), BF16),
+            pltpu.VMEM((count, HD, full), BF16),
+            pltpu.VMEM((count, reqs + 1, TREE, HD), BF16),
+            pltpu.VMEM((others, reqs + 1, TREE, HD), BF16),
+            pltpu.VMEM((count, rows, HD), BF16),
+            pltpu.VMEM((pairs - 1, rows, some), BF16),
+            pltpu.VMEM((pairs - 1, rows, some), BF16),
             pltpu.VMEM((8, HD), F32),
             pltpu.VMEM((others, 8, HD), F32),
-            dma((4 + 2 * reqs,)),
-            dma((pairs,)),
-            dma((others,)),
-            dma((others,)),
+            dma((7 + 2 * reqs,)),
+            dma((pairs + 1,)),
             dma((others,)),
             dma((others,)),
             dma((others,)),
             dma((others,)),
             dma((pairs,)),
             dma((pairs,)),
-            dma((1,)),
-            dma((1,)),
+            dma((others,)),
+            dma((others,)),
+            dma((others,)),
+            dma((others,)),
             dma((pairs - 1,)),
             dma((pairs - 1,)),
             dma((others,)),
             dma((others,)),
+            dma((2,)),
         ],
         compiler_params=pltpu.CompilerParams(
             collective_id=0, has_side_effects=True, vmem_limit_bytes=56 * 2**20
@@ -403,11 +491,20 @@
         v_tree,
         residual,
         wo_rows,
-        gain.reshape(1, cols),
+        gain.reshape(cols // HD, HD),
         parents,
         cache_len,
         accepted_node,
     )
+    layer_out, draft_feat = pl.pallas_call(
+        hand_over,
+        out_shape=out_shape,
+        in_specs=[hbm] * 2,
+        out_specs=(hbm, hbm),
+        scratch_shapes=[dma((2,))],
+        name="hand_over",
+    )(*results)
+    return layer_out, draft_feat.reshape(reqs, MAXACC, cols)
 
 
 def solution(mesh):

time: 34.6 us -> 37 us (1.069)
  Pallas kernels: 29.4 us -> 36.1 us
  local copies, waits for them, and re-layouts: 4.32 us -> 0 us
    pallas_call x1 -> x2, Pallas kernels: 29.4 us -> 36.1 us  [the longest x1 29 us: on_device(): pl.pallas_call(functools.partial(kernel, count), out_shape=out_shape, in_...]
    unnamed x2 -> x0, local copies, waits for them, and re-layouts: 3.04 us -> none
    reshape x1 -> x0, local copies, waits for them, and re-layouts: 1.28 us -> none  [on_device(): gain.reshape(1, cols)]
where the time goes in v2:
time: 37 us; the launch traced here: 36.7 us
  Pallas kernels  36.1 us (98%)
  between operations  0.64 us (2%)
    pallas_call x1, Pallas kernels, on_device(): pl.pallas_call(functools.partial(kernel, count), out_shape=out_shape, in_...  29 us
    pallas_call x1, Pallas kernels, on_device(): pl.pallas_call(hand_over, out_shape=out_shape, in_specs=[hbm] * 2, out_sp...  7.08 us

profile of v2, /device:TPU:0, one launch (start us, length us, event | category | flops | bytes accessed | tf_op | source)
XLA Modules:
  0.0 36.7 jit_solution(232534570295015667)
XLA Ops:
  0.6 29.0 %verify.1 = (bf16[64,1024]{1,0:T(8,128)(2,1)}, bf16[32,1024]{1,0:T(8,128)(2,1)}) custom-call(bf16[4,16,128]{2,1,0:T(8,128)(2,1)} %bitcast.3, bf16[4,256,512]{2,1,0:T(8,128)(2,1)} %k_ref.1, bf16[4,256,512]{2,1,0:T(8,128)(2,1)} %v_ref.1, bf16[4,16,512]{2,1,0:T(8,128)(2,1)} %kt_ref.1, bf16[4,16,512]{2,1,0:T(8,128)(2,1)} %vt_ref.1, bf16[64,1024]{1,0:T(8,128)(2,1)} %res_ref.1, ...), custom_call_target="tpu_custom_call" | custom-call | tf_op jit(solution)/shard_map/verify/pallas_call | solution.py:438
  29.6 7.1 %hand_over.1 = (bf16[64,1024]{1,0:T(8,128)(2,1)}, bf16[32,1024]{1,0:T(8,128)(2,1)}) custom-call(bf16[64,1024]{1,0:T(8,128)(2,1)} %get-tuple-element.6.out_in, bf16[32,1024]{1,0:T(8,128)(2,1)} %get-tuple-element.7.draft_in), custom_call_target="tpu_custom_call" | custom-call | tf_op jit(solution)/shard_map/hand_over/pallas_call | solution.py:499
